TPU v7x, 512 devices: a whole 4x8x8 slice. The times are simulated.
512 devices in a mesh: ctx: 64 (over z, y_hi, core), head: 8 (over x, y_lo).
Axes of the slice: x: 4, y: 8 (y_hi: 4, y_lo: 2; y = y_hi * 2 + y_lo), z: 8, core: 2. Of those that a mesh axis runs over, the one named last changes fastest.
Arguments:
- query_rows: bfloat16 [32768, 4096], P('ctx', 'head'), may hold values from -43 to 43
- key_rows: bfloat16 [32768, 4096], P('ctx', 'head'), may hold values from -4 to 4
- value_rows: bfloat16 [32768, 4096], P('ctx', 'head'), may hold values from -16 to 16
- out_gain: float32 [4096], P('head'), may hold values from 0.5 to 1.5
Outputs:
- normed: bfloat16 [32768, 4096], P('ctx', 'head')
All inputs are finite; a program needn't handle non-finite values.
Results may differ from a plain program's by a relative error of at most 0.0085.
Values may be sent and summed in bfloat16 or wider, within the bound.
No kernel may reach another device: no remote copies, remote signals or barrier semaphores. Data moves between devices by JAX's collectives and lax.ppermute only.
A program may use at most 64 MiB of HBM per device.

v0:
```python
import math
import jax
import jax.numpy as jnp
from jax import lax
from jax.sharding import PartitionSpec as P

HEADS = 32
HEAD_DIM = 128
BLOCK = 256
SUMMARY = 16


def band_block(block_items):
    query_part, key_part, value_part = block_items
    scores = jnp.einsum(
        "qhd,khd->hqk", query_part, key_part, preferred_element_type=jnp.float32
    ) * HEAD_DIM ** (-0.5)
    causal = lax.broadcasted_iota(jnp.int32, (BLOCK, BLOCK), 0) >= lax.broadcasted_iota(
        jnp.int32, (BLOCK, BLOCK), 1
    )
    scores = jnp.where(causal[None], scores, -1e30)
    row_max = jnp.max(scores, axis=-1)
    weights = jnp.where(causal[None], jnp.exp(scores - row_max[..., None]), 0.0)
    row_sum = jnp.sum(weights, axis=-1)
    joint_acc = jnp.einsum(
        "hqk,khd->qhd", weights.astype(jnp.bfloat16), value_part, preferred_element_type=jnp.float32
    )
    return (row_max, row_sum, joint_acc)


def summary_update(run_state, query_set, set_blocks, key_sub, value_sub, first_row):
    sub_rows = key_sub.shape[0]
    key_block = (first_row + jnp.arange(sub_rows, dtype=jnp.int32)) // SUMMARY

    def update(group_state):
        old_max, old_sum, old_acc = group_state
        scores = jnp.einsum(
            "gqhd,khd->ghqk", query_set, key_sub, preferred_element_type=jnp.float32
        ) * HEAD_DIM ** (-0.5)
        allowed = (key_block[None, :] < set_blocks[:, None])[:, None, None, :]
        scores = jnp.where(allowed, scores, -1e30)
        joint_max = jnp.maximum(old_max, jnp.max(scores, axis=-1))
        weights = jnp.where(allowed, jnp.exp(scores - joint_max[..., None]), 0.0)
        shrink = jnp.exp(old_max - joint_max)
        new_sum = old_sum * shrink + jnp.sum(weights, axis=-1)
        new_acc = old_acc * jnp.transpose(shrink, (0, 2, 1))[..., None] + jnp.einsum(
            "ghqk,khd->gqhd",
            weights.astype(jnp.bfloat16),
            value_sub,
            preferred_element_type=jnp.float32,
        )
        return (joint_max, new_sum, new_acc)

    def unchanged(group_state):
        return group_state

    return lax.cond(first_row // SUMMARY < jnp.max(set_blocks), update, unchanged, run_state)


def sweep_rows(run_state, query_set, set_blocks, key_part, value_part):
    piece_rows, head_count = (key_part.shape[0], key_part.shape[1])
    sub_rows = math.gcd(piece_rows, 512)
    sub_count = piece_rows // sub_rows
    key_split = key_part.reshape(sub_count, sub_rows, head_count, HEAD_DIM)
    value_split = value_part.reshape(sub_count, sub_rows, head_count, HEAD_DIM)
    first_rows = jnp.arange(sub_count, dtype=jnp.int32) * sub_rows

    def inner(state, sub_items):
        key_sub, value_sub, first_row = sub_items
        return (summary_update(state, query_set, set_blocks, key_sub, value_sub, first_row), None)

    run_state, _ = lax.scan(inner, run_state, (key_split, value_split, first_rows))
    return run_state


def summary_pass(query_set, set_blocks, summary_keys, summary_values):
    group_count, _, head_count, _ = query_set.shape
    initial = (
        jnp.full((group_count, head_count, BLOCK), -1e30, jnp.float32),
        jnp.zeros((group_count, head_count, BLOCK), jnp.float32),
        jnp.zeros((group_count, BLOCK, head_count, HEAD_DIM), jnp.float32),
    )
    return sweep_rows(
        initial,
        query_set,
        set_blocks,
        lax.all_gather(summary_keys, "ctx", axis=0, tiled=True),
        lax.all_gather(summary_values, "ctx", axis=0, tiled=True),
    )


def local(query_rows, key_rows, value_rows, out_gain):
    row_count, width = query_rows.shape
    head_count = width // HEAD_DIM
    block_count = row_count // BLOCK
    my_index = lax.axis_index("ctx")
    block_shape = (block_count, BLOCK, head_count, HEAD_DIM)
    query_blocks = query_rows.reshape(block_shape)
    key_blocks = key_rows.reshape(block_shape)
    value_blocks = value_rows.reshape(block_shape)
    band_max, band_sum, band_acc = lax.map(band_block, (query_blocks, key_blocks, value_blocks))
    summary_keys = key_blocks[:, BLOCK - SUMMARY :].reshape(
        block_count * SUMMARY, head_count, HEAD_DIM
    )
    summary_values = value_blocks[:, BLOCK - SUMMARY :].reshape(
        block_count * SUMMARY, head_count, HEAD_DIM
    )
    local_blocks = my_index * block_count + jnp.arange(block_count, dtype=jnp.int32)
    summary_state = summary_pass(query_blocks, local_blocks, summary_keys, summary_values)
    far_max, far_sum, far_acc = summary_state
    joint_max = jnp.maximum(band_max, far_max)
    band_scale = jnp.exp(band_max - joint_max)
    far_scale = jnp.exp(far_max - joint_max)
    joint_sum = band_sum * band_scale + far_sum * far_scale
    joint_acc = (
        band_acc * jnp.transpose(band_scale, (0, 2, 1))[..., None]
        + far_acc * jnp.transpose(far_scale, (0, 2, 1))[..., None]
    )
    attended = joint_acc / jnp.transpose(joint_sum, (0, 2, 1))[..., None]
    attended = attended.reshape(row_count, width)
    squares = jnp.sum(attended * attended, axis=-1)
    row_totals = lax.psum(squares, "head")
    row_scale = lax.rsqrt(row_totals / (HEADS * HEAD_DIM) + 1e-06)
    return (attended * row_scale[:, None] * out_gain).astype(jnp.bfloat16)


def solution(mesh):
    placed = (P("ctx", "head"), P("ctx", "head"), P("ctx", "head"), P("head"))
    return jax.shard_map(
        local, mesh=mesh, in_specs=placed, out_specs=P("ctx", "head"), check_vma=False
    )
```

profile of v0, /device:TPU:464, one launch (start us, length us, event | category | flops | bytes accessed | tf_op | source)
XLA Modules:
  0.0 243.3 jit_solution(7592375874192132577)
XLA Ops:
  6.5 1.2 reshape.64
  7.7 0.6 copy.24
  8.4 2.0 reshape.65
  10.4 0.8 slice.9
  11.1 0.6 copy.25
  11.8 0.6 add_reduce_fusion
  12.4 1.2 reshape.63
  13.7 1.1 broadcast.81.clone3
  14.8 7.0 %while.32 = (s32[]{:T(128)}, f32[2,4,256]{2,0,1:T(2,128)S(1)}, f32[2,4,256]{2,0,1:T(2,128)S(1)}, f32[2,256,4,128]{3,1,0,2:T(8,128)}, bf16[2,256,4,128]{3,2,1,0:T...) while((s32[]{:T(128)}, f32[2,4,256]{2,0,1:T(2,128)S(1)}, ...), condition=%wide.region_3.4_spmd, body=%wide.region_0.3_spmd.sunk | while | flops 136640512 | bytes 8962169 | solution.py:101
  14.9 1.1 constant_dynamic-slice_fusion.5
  16.8 0.3 convolution_bitcast_fusion.2
  17.4 0.9 constant_dynamic-update-slice_fusion.2
  18.4 1.1 constant_dynamic-slice_fusion.5
  20.9 0.9 constant_dynamic-update-slice_fusion.2
  21.8 66.8 %all-gather.3.cloned.1.call-done = bf16[2048,4,128]{2,0,1:T(8,128)(2,1)} async-done(((bf16[32,4,128]{2,0,1:T(8,128)(2,1)}), bf16[2048,4,128]{2,0,1:T(8,128)(2,1)}) %all-gather.3.cloned.1.call-update) | async-done | bytes 2097168 | tf_op jit(solution)/shard_map/all_gather | solution.py:87
  88.6 1.7 copy.26
  90.3 78.9 %all-gather.5.cloned.1.call-done = bf16[2048,4,128]{2,0,1:T(8,128)(2,1)} async-done(((bf16[32,4,128]{2,0,1:T(8,128)(2,1)}), bf16[2048,4,128]{2,0,1:T(8,128)(2,1)}) %all-gather.5.cloned.1.call-update) | async-done | bytes 2097168 | tf_op jit(solution)/shard_map/all_gather | solution.py:88
  169.2 3.1 %copy.28 = bf16[4,512,4,128]{3,1,2,0:T(8,128)(2,1)} copy(bf16[4,512,4,128]{3,1,0,2:T(8,128)(2,1)} %bitcast.98) | data formatting | bytes 4194304
  172.3 1.1 broadcast.81.clone3.1
  173.4 40.3 %while.33 = (s32[]{:T(128)}, f32[2,4,256]{2,0,1:T(2,128)S(1)}, f32[2,4,256]{2,0,1:T(2,128)S(1)}, f32[2,256,4,128]{3,1,0,2:T(8,128)}, s32[4]{0:T(128)S(1)}, /*ind...) while((s32[]{:T(128)}, f32[2,4,256]{2,0,1:T(2,128)S(1)}, ...), condition=%wide.region_10.11_spmd.clone, body=%wide.region_5.10_spmd.clone.sunk | while | flops 551042048 | bytes 24787012 | solution.py:72
  173.4 0.6 dynamic_slice.60
  177.2 6.2 %conditional.3 = ((f32[2,4,256]{2,0,1:T(2,128)S(1)}, f32[2,4,256]{2,0,1:T(2,128)S(1)}, f32[2,256,4,128]{3,1,0,2:T(8,128)})) conditional(s32[]{:T(128)} %convert_element_type.34, (f32[2,4,256]{2,0,1:T(2,128)S(1)}, f32[2,4,256]{2,0,1:T(2,128)S(1)}, f32[2,256,4,128]{3,1,0,2:T(8,128)}) %tuple.82, (s32[]{:T(128)}, s32[512]{0:T(512)S(1)}, s32[]{:T(128)}, ...), branch_computations={%region_6.6_spmd, %region_7.9_spmd.clone} | conditional | flops 551042048 | bytes 24784512 | solution.py:57
  177.2 0.7 add_select_fusion
  178.1 1.0 fusion.11
  179.1 3.2 %fusion.20 = f32[2,256,4,128]{3,1,0,2:T(8,128)S(1)} fusion(f32[4,512,2,256]{3,1,2,0:T(8,128)S(1)} %get-tuple-element.523, f32[2,4,256]{2,0,1:T(2,128)S(1)} %get-tuple-element.648, pred[2,512]{1,0:T(4,128)(4,1)S(1)} %broadcast_compare_fusion, f32[2,256,4,128]{3,1,0,2:T(8,128)S(1)} %copy-done, bf16[4,512,4,128]{3,1,2,0:T(8,128)(2,1)} %get-tuple-element.410, ...), kind=kOutput, calls=%fused_computation.27 | convolution fusion | flops 274202624 | bytes 6833664 | tf_op jit(solution)/shard_map/while/body/eval_jaxpr/cond/branch_1_fun/ghqk,khd->gqhd/dot_general | solution.py:46
  182.3 1.1 fusion.13
  183.5 0.6 dynamic_slice.60
  187.3 6.2 %conditional.3 = ((f32[2,4,256]{2,0,1:T(2,128)S(1)}, f32[2,4,256]{2,0,1:T(2,128)S(1)}, f32[2,256,4,128]{3,1,0,2:T(8,128)})) conditional(s32[]{:T(128)} %convert_element_type.34, (f32[2,4,256]{2,0,1:T(2,128)S(1)}, f32[2,4,256]{2,0,1:T(2,128)S(1)}, f32[2,256,4,128]{3,1,0,2:T(8,128)}) %tuple.82, (s32[]{:T(128)}, s32[512]{0:T(512)S(1)}, s32[]{:T(128)}, ...), branch_computations={%region_6.6_spmd, %region_7.9_spmd.clone} | conditional | flops 551042048 | bytes 24784512 | solution.py:57
  187.3 0.7 add_select_fusion
  188.1 1.0 fusion.11
  189.2 3.2 %fusion.20 = f32[2,256,4,128]{3,1,0,2:T(8,128)S(1)} fusion(f32[4,512,2,256]{3,1,2,0:T(8,128)S(1)} %get-tuple-element.523, f32[2,4,256]{2,0,1:T(2,128)S(1)} %get-tuple-element.648, pred[2,512]{1,0:T(4,128)(4,1)S(1)} %broadcast_compare_fusion, f32[2,256,4,128]{3,1,0,2:T(8,128)S(1)} %copy-done, bf16[4,512,4,128]{3,1,2,0:T(8,128)(2,1)} %get-tuple-element.410, ...), kind=kOutput, calls=%fused_computation.27 | convolution fusion | flops 274202624 | bytes 6833664 | tf_op jit(solution)/shard_map/while/body/eval_jaxpr/cond/branch_1_fun/ghqk,khd->gqhd/dot_general | solution.py:46
  192.4 1.1 fusion.13
  193.6 0.6 dynamic_slice.60
  197.4 6.2 %conditional.3 = ((f32[2,4,256]{2,0,1:T(2,128)S(1)}, f32[2,4,256]{2,0,1:T(2,128)S(1)}, f32[2,256,4,128]{3,1,0,2:T(8,128)})) conditional(s32[]{:T(128)} %convert_element_type.34, (f32[2,4,256]{2,0,1:T(2,128)S(1)}, f32[2,4,256]{2,0,1:T(2,128)S(1)}, f32[2,256,4,128]{3,1,0,2:T(8,128)}) %tuple.82, (s32[]{:T(128)}, s32[512]{0:T(512)S(1)}, s32[]{:T(128)}, ...), branch_computations={%region_6.6_spmd, %region_7.9_spmd.clone} | conditional | flops 551042048 | bytes 24784512 | solution.py:57
  197.4 0.7 add_select_fusion
  198.2 1.0 fusion.11
  199.2 3.2 %fusion.20 = f32[2,256,4,128]{3,1,0,2:T(8,128)S(1)} fusion(f32[4,512,2,256]{3,1,2,0:T(8,128)S(1)} %get-tuple-element.523, f32[2,4,256]{2,0,1:T(2,128)S(1)} %get-tuple-element.648, pred[2,512]{1,0:T(4,128)(4,1)S(1)} %broadcast_compare_fusion, f32[2,256,4,128]{3,1,0,2:T(8,128)S(1)} %copy-done, bf16[4,512,4,128]{3,1,2,0:T(8,128)(2,1)} %get-tuple-element.410, ...), kind=kOutput, calls=%fused_computation.27 | convolution fusion | flops 274202624 | bytes 6833664 | tf_op jit(solution)/shard_map/while/body/eval_jaxpr/cond/branch_1_fun/ghqk,khd->gqhd/dot_general | solution.py:46
  202.5 1.1 fusion.13
  203.6 0.6 dynamic_slice.60
  207.4 6.2 %conditional.3 = ((f32[2,4,256]{2,0,1:T(2,128)S(1)}, f32[2,4,256]{2,0,1:T(2,128)S(1)}, f32[2,256,4,128]{3,1,0,2:T(8,128)})) conditional(s32[]{:T(128)} %convert_element_type.34, (f32[2,4,256]{2,0,1:T(2,128)S(1)}, f32[2,4,256]{2,0,1:T(2,128)S(1)}, f32[2,256,4,128]{3,1,0,2:T(8,128)}) %tuple.82, (s32[]{:T(128)}, s32[512]{0:T(512)S(1)}, s32[]{:T(128)}, ...), branch_computations={%region_6.6_spmd, %region_7.9_spmd.clone} | conditional | flops 551042048 | bytes 24784512 | solution.py:57
  207.5 0.7 add_select_fusion
  208.3 1.0 fusion.11
  209.3 3.2 %fusion.20 = f32[2,256,4,128]{3,1,0,2:T(8,128)S(1)} fusion(f32[4,512,2,256]{3,1,2,0:T(8,128)S(1)} %get-tuple-element.523, f32[2,4,256]{2,0,1:T(2,128)S(1)} %get-tuple-element.648, pred[2,512]{1,0:T(4,128)(4,1)S(1)} %broadcast_compare_fusion, f32[2,256,4,128]{3,1,0,2:T(8,128)S(1)} %copy-done, bf16[4,512,4,128]{3,1,2,0:T(8,128)(2,1)} %get-tuple-element.410, ...), kind=kOutput, calls=%fused_computation.27 | convolution fusion | flops 274202624 | bytes 6833664 | tf_op jit(solution)/shard_map/while/body/eval_jaxpr/cond/branch_1_fun/ghqk,khd->gqhd/dot_general | solution.py:46
  212.6 1.1 fusion.13
  213.7 2.4 multiply_reduce_fusion
  216.1 18.7 %psum.7 = f32[512]{0:T(512)S(1)} all-reduce(f32[512]{0:T(512)S(1)} %bitcast.107), channel_id=1, replica_groups=mesh['ctx'=64,'head'=8] {'head'}, use_global_device_ids=true, to_apply=%region_12.13 | all-reduce | flops 512 | bytes 4096 | tf_op jit(solution)/shard_map/psum | solution.py:122
  234.8 0.7 copy.33
  235.5 0.9 fusion.37
  (81 shorter events, 3.3 us)
Async XLA Ops:
  6.5 82.0 %all-gather.3.cloned.1.call-start = ((), (), s32[]{:S(2)}) async-start(), calls=%async_computation | async-start | bytes 2129920 | tf_op jit(solution)/shard_map/all_gather | solution.py:87
  8.4 160.9 %all-gather.5.cloned.1.call-start = ((), (), s32[]{:S(2)}) async-start(), calls=%async_computation.1 | async-start | bytes 2129920 | tf_op jit(solution)/shard_map/all_gather | solution.py:88
  177.2 1.8 copy-start
  182.3 1.1 copy-start.1
  187.3 1.8 copy-start
  192.4 1.1 copy-start.1
  197.4 1.8 copy-start
  202.5 1.1 copy-start.1
  207.5 1.8 copy-start
  212.5 1.1 copy-start.1
  213.7 21.8 %copy-start.2 = (f32[512]{0:T(512)S(1)}, f32[512]{0:T(512)}, u32[]{:S(2)}) copy-start(f32[512]{0:T(512)} %param.13) | copy-start | bytes 6148
Sparse Core Ops, SparseCore 0:
  10.6 77.9 all-gather.2
  91.8 77.3 all-gather.4
where the time goes:
time: 244 us; the launch traced here: 243 us
  waiting for transfers between devices  146 us (60%)
  local copies, waits for them, and re-layouts  21.7 us (9%)
  blocking collectives  18.7 us (8%)
  matrix products  18.1 us (7%)
  between operations  13.5 us (6%)
  loops' own time  13.4 us (5%)
  other arithmetic  12.1 us (5%)
    all_gather x1, waiting for transfers between devices, summary_pass(): lax.all_gather(summary_values, 'ctx', axis=0, tiled=True)  78.9 us
    all_gather x1, waiting for transfers between devices, summary_pass(): lax.all_gather(summary_keys, 'ctx', axis=0, tiled=True)  66.8 us
    psum x1, blocking collectives, local(): row_totals = lax.psum(squares, 'head')  18.7 us
    dot_general x4, matrix products, update(): jnp.einsum('ghqk,khd->gqhd', weights.astype(jnp.bfloat16), value_sub, pre...  12.9 us
    another operation x1, loops' own time, sweep_rows(): lax.scan(inner, run_state, (key_split, value_split, first_rows))  12.8 us
    unnamed x6, local copies, waits for them, and re-layouts  4.9 us
  transfers between devices with their start and end apart: 2, of which 2 were waited for; matrix products, arithmetic and copies ran while one was open for 6% of the time, Pallas kernels for 0%

commit v1 on v0

--- a/solution.py
+++ b/solution.py
@@ -84,7 +84,9 @@
         initial,
         query_set,
         set_blocks,
-        lax.all_gather(summary_keys, "ctx", axis=0, tiled=True),
+        jnp.concatenate(
+            lax.all_to_all(jnp.stack([summary_keys] * lax.axis_size("ctx")), "ctx", 0, 0), axis=0
+        ),
         lax.all_gather(summary_values, "ctx", axis=0, tiled=True),
     )
 

time: 244 us -> 205 us (0.84)
  waiting for transfers between devices: 146 us -> 93.2 us
  starting transfers between devices: 0.04 us -> 10.6 us
    all_gather x1 -> x0, waiting for transfers between devices: 66.8 us -> none  [summary_pass(): lax.all_gather(summary_keys, 'ctx', axis=0, tiled=True)]
    all_gather x1, waiting for transfers between devices: 78.9 us -> 93.2 us  [summary_pass(): lax.all_gather(summary_values, 'ctx', axis=0, tiled=True)]
    all_to_all x0 -> x1, starting transfers between devices: none -> 10.6 us  [summary_pass(): lax.all_to_all(jnp.stack([summary_keys] * lax.axis_size('ctx')), 'ctx', 0...]
    unnamed x6 -> x8, local copies, waits for them, and re-layouts: 4.9 us -> 3.37 us
  transfers between devices with their start and end apart: 2 -> 2, of which waited for: 2 -> 1; matrix products, arithmetic and copies ran while one was open for 6% -> 8% of each run, Pallas kernels for 0% -> 0%
where the time goes in v1:
time: 205 us; the launch traced here: 204 us
  waiting for transfers between devices  93.2 us (45%)
  local copies, waits for them, and re-layouts  22.7 us (11%)
  blocking collectives  18.7 us (9%)
  matrix products  18.1 us (9%)
  loops' own time  14.5 us (7%)
  between operations  13.6 us (7%)
  other arithmetic  12.4 us (6%)
  starting transfers between devices  10.6 us (5%)
    all_gather x1, waiting for transfers between devices, summary_pass(): lax.all_gather(summary_values, 'ctx', axis=0, tiled=True)  93.2 us
    psum x1, blocking collectives, local(): row_totals = lax.psum(squares, 'head')  18.7 us
    another operation x1, loops' own time, sweep_rows(): lax.scan(inner, run_state, (key_split, value_split, first_rows))  14 us
    dot_general x4, matrix products, update(): jnp.einsum('ghqk,khd->gqhd', weights.astype(jnp.bfloat16), value_sub, pre...  12.9 us
    all_to_all x1, starting transfers between devices, summary_pass(): lax.all_to_all(jnp.stack([summary_keys] * lax.axis_size('ctx')), 'ctx', 0...  10.6 us
    reduce_sum x4, other arithmetic, update(): new_sum = old_sum * shrink + jnp.sum(weights, axis=-1)  4.33 us
  transfers between devices with their start and end apart: 2, of which 1 were waited for; matrix products, arithmetic and copies ran while one was open for 8% of the time, Pallas kernels for 0%

profile of v1, /device:TPU:464, one launch (start us, length us, event | category | flops | bytes accessed | tf_op | source)
XLA Modules:
  0.0 203.8 jit_solution(961679591313654301)
XLA Ops:
  6.5 1.2 reshape.61
  7.8 0.6 copy.44
  8.4 2.0 reshape.60
  10.4 0.8 slice.8
  11.2 1.8 stack.3
  13.0 10.6 %all-to-all-start = ((bf16[64,32,4,128]{3,1,2,0:T(8,128)(2,1)}), bf16[64,32,4,128]{3,1,2,0:T(8,128)(2,1)}, u32[]{:S(2)}, u32[]{:S(2)}) async-start(bf16[64,32,4,128]{3,1,2,0:T(8,128)(2,1)} %stack.3), calls=%async_computation | async-start | bytes 4194304 | tf_op jit(solution)/shard_map/all_to_all | solution.py:88
  23.6 0.7 add_reduce_fusion
  24.5 1.2 broadcast.82.clone3
  25.7 7.1 %while.32 = (s32[]{:T(128)}, f32[2,4,256]{2,0,1:T(2,128)S(1)}, f32[2,4,256]{2,0,1:T(2,128)S(1)}, f32[2,256,4,128]{3,1,0,2:T(8,128)}, bf16[2,256,4,128]{3,2,1,0:T...) while((s32[]{:T(128)}, f32[2,4,256]{2,0,1:T(2,128)S(1)}, ...), condition=%wide.region_3.4_spmd, body=%wide.region_0.3_spmd.sunk | while | flops 136640512 | bytes 8962169 | solution.py:103
  25.8 1.1 constant_dynamic-slice_fusion.5
  27.8 0.3 convolution_bitcast_fusion.2
  28.4 0.9 constant_dynamic-update-slice_fusion.2
  29.4 1.1 constant_dynamic-slice_fusion.5
  31.3 0.3 convolution_bitcast_fusion.2
  31.9 0.9 constant_dynamic-update-slice_fusion.2
  32.8 93.2 %all-gather.2.cloned.1.call-done = bf16[2048,4,128]{2,0,1:T(8,128)(2,1)} async-done(((bf16[32,4,128]{2,0,1:T(8,128)(2,1)}), bf16[2048,4,128]{2,0,1:T(8,128)(2,1)}) %all-gather.2.cloned.1.call-update) | async-done | bytes 2097168 | tf_op jit(solution)/shard_map/all_gather | solution.py:90
  125.9 3.1 %copy.47 = bf16[4,512,4,128]{3,1,2,0:T(8,128)(2,1)} copy(bf16[4,512,4,128]{3,1,0,2:T(8,128)(2,1)} %bitcast.98) | data formatting | bytes 4194304
  129.1 2.0 copy.43
  131.3 1.1 broadcast.82.clone3.1
  132.3 41.8 %while.33 = (s32[]{:T(128)}, f32[2,4,256]{2,0,1:T(2,128)S(1)}, f32[2,4,256]{2,0,1:T(2,128)S(1)}, f32[2,256,4,128]{3,1,0,2:T(8,128)}, s32[4]{0:T(128)S(1)}, /*ind...) while((s32[]{:T(128)}, f32[2,4,256]{2,0,1:T(2,128)S(1)}, ...), condition=%wide.region_10.11_spmd.clone, body=%wide.region_5.10_spmd.clone.sunk | while | flops 551042048 | bytes 24787012 | solution.py:72
  132.3 0.7 dynamic_slice.60
  136.5 6.3 %conditional.3 = ((f32[2,4,256]{2,0,1:T(2,128)S(1)}, f32[2,4,256]{2,0,1:T(2,128)S(1)}, f32[2,256,4,128]{3,1,0,2:T(8,128)})) conditional(s32[]{:T(128)} %convert_element_type.34, (f32[2,4,256]{2,0,1:T(2,128)S(1)}, f32[2,4,256]{2,0,1:T(2,128)S(1)}, f32[2,256,4,128]{3,1,0,2:T(8,128)}) %tuple.84, (s32[]{:T(128)}, s32[512]{0:T(512)S(1)}, s32[]{:T(128)}, ...), branch_computations={%region_6.6_spmd, %region_7.9_spmd.clone} | conditional | flops 551042048 | bytes 24784512 | solution.py:57
  136.5 0.8 add_select_fusion
  137.4 1.0 fusion.11
  138.4 3.2 %fusion.20 = f32[2,256,4,128]{3,1,0,2:T(8,128)S(1)} fusion(f32[4,512,2,256]{3,1,2,0:T(8,128)S(1)} %get-tuple-element.540, f32[2,4,256]{2,0,1:T(2,128)S(1)} %get-tuple-element.665, pred[2,512]{1,0:T(4,128)(4,1)S(1)} %broadcast_compare_fusion, f32[2,256,4,128]{3,1,0,2:T(8,128)S(1)} %copy-done, bf16[4,512,4,128]{3,1,2,0:T(8,128)(2,1)} %get-tuple-element.410, ...), kind=kOutput, calls=%fused_computation.27 | convolution fusion | flops 274202624 | bytes 6833664 | tf_op jit(solution)/shard_map/while/body/eval_jaxpr/cond/branch_1_fun/ghqk,khd->gqhd/dot_general | solution.py:46
  141.6 1.1 fusion.13
  142.8 0.7 dynamic_slice.60
  146.9 6.3 %conditional.3 = ((f32[2,4,256]{2,0,1:T(2,128)S(1)}, f32[2,4,256]{2,0,1:T(2,128)S(1)}, f32[2,256,4,128]{3,1,0,2:T(8,128)})) conditional(s32[]{:T(128)} %convert_element_type.34, (f32[2,4,256]{2,0,1:T(2,128)S(1)}, f32[2,4,256]{2,0,1:T(2,128)S(1)}, f32[2,256,4,128]{3,1,0,2:T(8,128)}) %tuple.84, (s32[]{:T(128)}, s32[512]{0:T(512)S(1)}, s32[]{:T(128)}, ...), branch_computations={%region_6.6_spmd, %region_7.9_spmd.clone} | conditional | flops 551042048 | bytes 24784512 | solution.py:57
  147.0 0.8 add_select_fusion
  147.8 1.0 fusion.11
  148.9 3.2 %fusion.20 = f32[2,256,4,128]{3,1,0,2:T(8,128)S(1)} fusion(f32[4,512,2,256]{3,1,2,0:T(8,128)S(1)} %get-tuple-element.540, f32[2,4,256]{2,0,1:T(2,128)S(1)} %get-tuple-element.665, pred[2,512]{1,0:T(4,128)(4,1)S(1)} %broadcast_compare_fusion, f32[2,256,4,128]{3,1,0,2:T(8,128)S(1)} %copy-done, bf16[4,512,4,128]{3,1,2,0:T(8,128)(2,1)} %get-tuple-element.410, ...), kind=kOutput, calls=%fused_computation.27 | convolution fusion | flops 274202624 | bytes 6833664 | tf_op jit(solution)/shard_map/while/body/eval_jaxpr/cond/branch_1_fun/ghqk,khd->gqhd/dot_general | solution.py:46
  152.1 1.1 fusion.13
  153.2 0.7 dynamic_slice.60
  157.4 6.3 %conditional.3 = ((f32[2,4,256]{2,0,1:T(2,128)S(1)}, f32[2,4,256]{2,0,1:T(2,128)S(1)}, f32[2,256,4,128]{3,1,0,2:T(8,128)})) conditional(s32[]{:T(128)} %convert_element_type.34, (f32[2,4,256]{2,0,1:T(2,128)S(1)}, f32[2,4,256]{2,0,1:T(2,128)S(1)}, f32[2,256,4,128]{3,1,0,2:T(8,128)}) %tuple.84, (s32[]{:T(128)}, s32[512]{0:T(512)S(1)}, s32[]{:T(128)}, ...), branch_computations={%region_6.6_spmd, %region_7.9_spmd.clone} | conditional | flops 551042048 | bytes 24784512 | solution.py:57
  157.4 0.8 add_select_fusion
  158.3 1.0 fusion.11
  159.3 3.2 %fusion.20 = f32[2,256,4,128]{3,1,0,2:T(8,128)S(1)} fusion(f32[4,512,2,256]{3,1,2,0:T(8,128)S(1)} %get-tuple-element.540, f32[2,4,256]{2,0,1:T(2,128)S(1)} %get-tuple-element.665, pred[2,512]{1,0:T(4,128)(4,1)S(1)} %broadcast_compare_fusion, f32[2,256,4,128]{3,1,0,2:T(8,128)S(1)} %copy-done, bf16[4,512,4,128]{3,1,2,0:T(8,128)(2,1)} %get-tuple-element.410, ...), kind=kOutput, calls=%fused_computation.27 | convolution fusion | flops 274202624 | bytes 6833664 | tf_op jit(solution)/shard_map/while/body/eval_jaxpr/cond/branch_1_fun/ghqk,khd->gqhd/dot_general | solution.py:46
  162.6 1.1 fusion.13
  163.7 0.7 dynamic_slice.60
  167.9 6.3 %conditional.3 = ((f32[2,4,256]{2,0,1:T(2,128)S(1)}, f32[2,4,256]{2,0,1:T(2,128)S(1)}, f32[2,256,4,128]{3,1,0,2:T(8,128)})) conditional(s32[]{:T(128)} %convert_element_type.34, (f32[2,4,256]{2,0,1:T(2,128)S(1)}, f32[2,4,256]{2,0,1:T(2,128)S(1)}, f32[2,256,4,128]{3,1,0,2:T(8,128)}) %tuple.84, (s32[]{:T(128)}, s32[512]{0:T(512)S(1)}, s32[]{:T(128)}, ...), branch_computations={%region_6.6_spmd, %region_7.9_spmd.clone} | conditional | flops 551042048 | bytes 24784512 | solution.py:57
  167.9 0.8 add_select_fusion
  168.8 1.0 fusion.11
  169.8 3.2 %fusion.20 = f32[2,256,4,128]{3,1,0,2:T(8,128)S(1)} fusion(f32[4,512,2,256]{3,1,2,0:T(8,128)S(1)} %get-tuple-element.540, f32[2,4,256]{2,0,1:T(2,128)S(1)} %get-tuple-element.665, pred[2,512]{1,0:T(4,128)(4,1)S(1)} %broadcast_compare_fusion, f32[2,256,4,128]{3,1,0,2:T(8,128)S(1)} %copy-done, bf16[4,512,4,128]{3,1,2,0:T(8,128)(2,1)} %get-tuple-element.410, ...), kind=kOutput, calls=%fused_computation.27 | convolution fusion | flops 274202624 | bytes 6833664 | tf_op jit(solution)/shard_map/while/body/eval_jaxpr/cond/branch_1_fun/ghqk,khd->gqhd/dot_general | solution.py:46
  173.0 1.1 fusion.13
  174.2 2.4 %multiply_reduce_fusion = (f32[2,256]{1,0:T(2,128)S(1)}, f32[2,256,4,128]{3,1,0,2:T(8,128)S(1)}) fusion(f32[2,256,4]{1,0,2:T(2,128)S(1)} %get-tuple-element.542, f32[2,256,4,128]{3,1,0,2:T(8,128)} %get-tuple-element.396, f32[2,256,4]{1,0,2:T(2,128)S(1)} %get-tuple-element.543, f32[2,256,4,128]{3,1,0,2:T(8,128)} %get-tuple-element.393, ...), kind=kLoop, calls=%fused_computation.53 | loop fusion | flops 1572352 | bytes 3172352 | tf_op jit(solution)/shard_map/reduce_sum | solution.py:123
  176.6 18.7 %psum.7 = f32[512]{0:T(512)S(1)} all-reduce(f32[512]{0:T(512)S(1)} %bitcast.107), channel_id=1, replica_groups=mesh['ctx'=64,'head'=8] {'head'}, use_global_device_ids=true, to_apply=%region_12.13 | all-reduce | flops 512 | bytes 4096 | tf_op jit(solution)/shard_map/psum | solution.py:124
  195.3 0.7 copy.52
  196.0 0.9 fusion.37
  (84 shorter events, 3.2 us)
Async XLA Ops:
  6.5 17.8 %copy-start.2 = (bf16[512,512]{1,0:T(8,128)(2,1)S(1)}, bf16[512,512]{1,0:T(8,128)(2,1)}, u32[]{:S(2)}) copy-start(bf16[512,512]{1,0:T(8,128)(2,1)} %param.10) | copy-start | bytes 1572868
  6.5 119.4 %all-gather.2.cloned.1.call-start = ((), (), s32[]{:S(2)}) async-start(), calls=%async_computation.1 | async-start | bytes 2129920 | tf_op jit(solution)/shard_map/all_gather | solution.py:90
  13.0 116.1 %all-to-all-start = ((bf16[64,32,4,128]{3,1,2,0:T(8,128)(2,1)}), bf16[64,32,4,128]{3,1,2,0:T(8,128)(2,1)}, u32[]{:S(2)}, u32[]{:S(2)}) async-start(bf16[64,32,4,128]{3,1,2,0:T(8,128)(2,1)} %stack.3), calls=%async_computation | async-start | bytes 4194304 | tf_op jit(solution)/shard_map/all_to_all | solution.py:88
  136.5 1.9 copy-start
  141.6 1.1 copy-start.1
  147.0 1.9 copy-start
  152.1 1.1 copy-start.1
  157.4 1.9 copy-start
  162.5 1.1 copy-start.1
  167.9 1.9 copy-start
  173.0 1.1 copy-start.1
  174.2 21.8 %copy-start.3 = (f32[512]{0:T(512)S(1)}, f32[512]{0:T(512)}, u32[]{:S(2)}) copy-start(f32[512]{0:T(512)} %param.13) | copy-start | bytes 6148
Sparse Core Ops, SparseCore 0:
  10.6 115.3 all-gather.1
